TPU v7x, 32 devices: a whole 2x2x4 slice. The times are simulated.
32 devices in a mesh: dp: 4 (over y, core), fsdp: 8 (over z, x).
Axes of the slice: x: 2, y: 2, z: 4, core: 2. Of those that a mesh axis runs over, the one named last changes fastest.
Arguments:
- frames: bfloat16 [16384, 768], P(('dp', 'fsdp')), may hold values from -6 to 6
- lengths: int32 [32, 2], P(('dp', 'fsdp')), may hold values from 0 to 512, as said below
- query_weight: bfloat16 [768, 768], P(('dp', 'fsdp')), may hold values from -0.21875 to 0.21875
- query_bias: bfloat16 [768], P(('dp', 'fsdp')), may hold values from -3 to 3
- key_weight: bfloat16 [768, 768], P(('dp', 'fsdp')), may hold values from -0.21875 to 0.21875
- value_weight: bfloat16 [768, 768], P(('dp', 'fsdp')), may hold values from -0.21875 to 0.21875
- value_bias: bfloat16 [768], P(('dp', 'fsdp')), may hold values from -3 to 3
- output_weight: bfloat16 [768, 768], P(('dp', 'fsdp')), may hold values from -2.5 to 2.5
- output_bias: bfloat16 [768], P(('dp', 'fsdp')), may hold values from -3 to 3
- first_gain: bfloat16 [768], P(('dp', 'fsdp')), may hold values from 0.5 to 1.5
- first_shift: bfloat16 [768], P(('dp', 'fsdp')), may hold values from -3 to 3
- inner_weight: bfloat16 [768, 3072], P(('dp', 'fsdp')), may hold values from -0.21875 to 0.21875
- inner_bias: bfloat16 [3072], P(('dp', 'fsdp')), may hold values from -3 to 3
- outer_weight: bfloat16 [3072, 768], P(('dp', 'fsdp')), may hold values from -0.109375 to 0.109375
- outer_bias: bfloat16 [768], P(('dp', 'fsdp')), may hold values from -3 to 3
- second_gain: bfloat16 [768], P(('dp', 'fsdp')), may hold values from 0.5 to 1.5
- second_shift: bfloat16 [768], P(('dp', 'fsdp')), may hold values from -3 to 3
- grad_out: bfloat16 [16384, 768], P(('dp', 'fsdp')), may hold values from -6 to 6
Outputs:
- layer_out: bfloat16 [16384, 768], P(('dp', 'fsdp'))
- frames_grad: bfloat16 [16384, 768], P(('dp', 'fsdp'))
- query_weight_grad: float32 [768, 768], P(('dp', 'fsdp'))
- query_bias_grad: float32 [768], P(('dp', 'fsdp'))
- key_weight_grad: float32 [768, 768], P(('dp', 'fsdp'))
- value_weight_grad: float32 [768, 768], P(('dp', 'fsdp'))
- value_bias_grad: float32 [768], P(('dp', 'fsdp'))
- output_weight_grad: float32 [768, 768], P(('dp', 'fsdp'))
- output_bias_grad: float32 [768], P(('dp', 'fsdp'))
- first_gain_grad: float32 [768], P(('dp', 'fsdp'))
- first_shift_grad: float32 [768], P(('dp', 'fsdp'))
- inner_weight_grad: float32 [768, 3072], P(('dp', 'fsdp'))
- inner_bias_grad: float32 [3072], P(('dp', 'fsdp'))
- outer_weight_grad: float32 [3072, 768], P(('dp', 'fsdp'))
- outer_bias_grad: float32 [768], P(('dp', 'fsdp'))
- second_gain_grad: float32 [768], P(('dp', 'fsdp'))
- second_shift_grad: float32 [768], P(('dp', 'fsdp'))
Inputs may be any that keep to these rules, and one draw needn't show every extreme that they name: `lengths`: row b holds block b's two utterances: slot 0 has 100 to 512 frames, slot 1 has 0 (empty) up to 512 minus slot 0; the block's remaining slots are padding. In one block, drawn from the seed, slot 0 fills all 512 slots.
All inputs are finite; a program needn't handle non-finite values.
Results may differ from a plain program's by a relative error of at most 0.015.
Values may be sent and summed in bfloat16 or wider, within the bound.
A program may use at most 192 MiB of HBM per device.

v0:
```python
import jax
import jax.numpy as jnp
from jax import lax
from jax.sharding import PartitionSpec as P

HEADS = 12


def layer_norm(values, gain_vec, shift_vec):
    center = values - jnp.mean(values, axis=-1, keepdims=True)
    spread = jnp.mean(center * center, axis=-1, keepdims=True)
    return center * lax.rsqrt(spread + 1e-05) * gain_vec + shift_vec


def exact_gelu(values):
    return jax.nn.gelu(values, approximate=False)


def matmul(left_side, right_side):
    return jnp.dot(left_side, right_side, preferred_element_type=jnp.float32)


def matmul_tn(left_side, right_side):
    return lax.dot_general(
        left_side, right_side, (((0,), (0,)), ((), ())), preferred_element_type=jnp.float32
    )


def matmul_nt(left_side, right_side):
    return lax.dot_general(
        left_side, right_side, (((1,), (1,)), ((), ())), preferred_element_type=jnp.float32
    )


def column_sums(values):
    return jnp.sum(values.astype(jnp.float32), axis=0)


def block_scores(query_block, key_heads, group_block, groups, score_scale):
    raw_scores = (
        jnp.einsum("qhd,khd->hqk", query_block, key_heads, preferred_element_type=jnp.float32)
        * score_scale
    )
    allowed = group_block[:, None] == groups[None, :]
    return jnp.where(allowed[None], raw_scores, -1e30)


def per_device(
    frames,
    lengths,
    query_weight,
    query_bias,
    key_weight,
    value_weight,
    value_bias,
    output_weight,
    output_bias,
    first_gain,
    first_shift,
    inner_weight,
    inner_bias,
    outer_weight,
    outer_bias,
    second_gain,
    second_shift,
    grad_out,
):
    frame_count = frames.shape[0]
    model_width = frames.shape[1]
    head_size = model_width // HEADS
    score_scale = head_size ** (-0.5)
    places = jnp.arange(frame_count, dtype=jnp.int32)
    bounds = jnp.stack([lengths[0, 0], lengths[0, 0] + lengths[0, 1]])
    groups = jnp.sum((places[:, None] >= bounds[None, :]).astype(jnp.int32), axis=1)
    live_mask = (places < bounds[-1]).astype(jnp.float32)
    gathered = (
        lax.all_gather(query_weight, ("dp", "fsdp"), axis=0, tiled=True),
        lax.all_gather(query_bias, ("dp", "fsdp"), axis=0, tiled=True),
        lax.all_gather(key_weight, ("dp", "fsdp"), axis=0, tiled=True),
        lax.all_gather(value_weight, ("dp", "fsdp"), axis=0, tiled=True),
        lax.all_gather(value_bias, ("dp", "fsdp"), axis=0, tiled=True),
        lax.all_gather(output_weight, ("dp", "fsdp"), axis=0, tiled=True),
        lax.all_gather(output_bias, ("dp", "fsdp"), axis=0, tiled=True),
        lax.all_gather(first_gain, ("dp", "fsdp"), axis=0, tiled=True),
        lax.all_gather(first_shift, ("dp", "fsdp"), axis=0, tiled=True),
        lax.all_gather(inner_weight, ("dp", "fsdp"), axis=0, tiled=True),
        lax.all_gather(inner_bias, ("dp", "fsdp"), axis=0, tiled=True),
        lax.all_gather(outer_weight, ("dp", "fsdp"), axis=0, tiled=True),
        lax.all_gather(outer_bias, ("dp", "fsdp"), axis=0, tiled=True),
        lax.all_gather(second_gain, ("dp", "fsdp"), axis=0, tiled=True),
        lax.all_gather(second_shift, ("dp", "fsdp"), axis=0, tiled=True),
    )
    (
        query_mat,
        query_vec,
        key_mat,
        value_mat,
        value_vec,
        output_mat,
        output_vec,
        first_scale,
        first_offset,
        inner_mat,
        inner_vec,
        outer_mat,
        outer_vec,
        second_scale,
        second_offset,
    ) = gathered
    query_rows = (matmul(frames, query_mat) + query_vec.astype(jnp.float32)).astype(jnp.bfloat16)
    key_rows = matmul(frames, key_mat).astype(jnp.bfloat16)
    value_rows = (matmul(frames, value_mat) + value_vec.astype(jnp.float32)).astype(jnp.bfloat16)
    query_heads = query_rows.reshape(frame_count, HEADS, head_size)
    key_heads = key_rows.reshape(frame_count, HEADS, head_size)
    value_heads = value_rows.reshape(frame_count, HEADS, head_size)
    scores = block_scores(query_heads, key_heads, groups, groups, score_scale)
    row_max = jnp.max(scores, axis=-1, keepdims=True)
    raw_weights = jnp.exp(scores - row_max)
    row_total = jnp.sum(raw_weights, axis=-1, keepdims=True)
    attn_prob = raw_weights / row_total
    log_totals = row_max + jnp.log(row_total)
    context_parts = jnp.einsum(
        "hqk,khd->qhd",
        attn_prob.astype(jnp.bfloat16),
        value_heads,
        preferred_element_type=jnp.float32,
    )
    context_rows = context_parts.reshape(frame_count, model_width).astype(jnp.bfloat16)
    frames_float = frames.astype(jnp.float32)
    resid_one = frames_float + matmul(context_rows, output_mat) + output_vec.astype(jnp.float32)
    hidden, first_pull = jax.vjp(
        layer_norm, resid_one, first_scale.astype(jnp.float32), first_offset.astype(jnp.float32)
    )
    hidden_low = hidden.astype(jnp.bfloat16)
    inner_pre = matmul(hidden_low, inner_mat) + inner_vec.astype(jnp.float32)
    active, gelu_pull = jax.vjp(exact_gelu, inner_pre)
    active_low = active.astype(jnp.bfloat16)
    outer_out = matmul(active_low, outer_mat) + outer_vec.astype(jnp.float32)
    normed_out, second_pull = jax.vjp(
        layer_norm,
        hidden + outer_out,
        second_scale.astype(jnp.float32),
        second_offset.astype(jnp.float32),
    )
    layer_out = (normed_out * live_mask[:, None]).astype(jnp.bfloat16)
    grad_top = grad_out.astype(jnp.float32) * live_mask[:, None]
    grad_two, second_gain_grad, second_shift_grad = second_pull(grad_top)
    grad_outer = grad_two.astype(jnp.bfloat16)
    outer_mat_grad = matmul_tn(active_low, grad_outer)
    outer_vec_grad = column_sums(grad_outer)
    (grad_inner,) = gelu_pull(matmul_nt(grad_outer, outer_mat))
    grad_inner_low = grad_inner.astype(jnp.bfloat16)
    inner_mat_grad = matmul_tn(hidden_low, grad_inner_low)
    inner_vec_grad = column_sums(grad_inner_low)
    grad_hidden = grad_two + matmul_nt(grad_inner_low, inner_mat)
    grad_one, first_gain_grad, first_shift_grad = first_pull(grad_hidden)
    grad_attn = grad_one.astype(jnp.bfloat16)
    output_mat_grad = matmul_tn(context_rows, grad_attn)
    output_vec_grad = column_sums(grad_attn)
    grad_context = (
        matmul_nt(grad_attn, output_mat).astype(jnp.bfloat16).reshape(frame_count, HEADS, head_size)
    )
    scores = block_scores(query_heads, key_heads, groups, groups, score_scale)
    attn_prob = jnp.exp(scores - log_totals)
    grad_prob = jnp.einsum(
        "qhd,khd->hqk", grad_context, value_heads, preferred_element_type=jnp.float32
    )
    inner_sum = jnp.sum(attn_prob * grad_prob, axis=-1, keepdims=True)
    grad_scores = (attn_prob * (grad_prob - inner_sum)).astype(jnp.bfloat16)
    query_grad_parts = (
        jnp.einsum("hqk,khd->qhd", grad_scores, key_heads, preferred_element_type=jnp.float32)
        * score_scale
    )
    key_grad_sum = (
        jnp.einsum("hqk,qhd->khd", grad_scores, query_heads, preferred_element_type=jnp.float32)
        * score_scale
    )
    value_grad_sum = jnp.einsum(
        "hqk,qhd->khd",
        attn_prob.astype(jnp.bfloat16),
        grad_context,
        preferred_element_type=jnp.float32,
    )
    grad_query = query_grad_parts.reshape(frame_count, model_width).astype(jnp.bfloat16)
    grad_key = key_grad_sum.reshape(frame_count, model_width).astype(jnp.bfloat16)
    grad_value = value_grad_sum.reshape(frame_count, model_width).astype(jnp.bfloat16)
    query_mat_grad = matmul_tn(frames, grad_query)
    query_vec_grad = column_sums(grad_query)
    key_mat_grad = matmul_tn(frames, grad_key)
    value_mat_grad = matmul_tn(frames, grad_value)
    value_vec_grad = column_sums(grad_value)
    frames_grad = (
        grad_one
        + matmul_nt(grad_query, query_mat)
        + matmul_nt(grad_key, key_mat)
        + matmul_nt(grad_value, value_mat)
    ).astype(jnp.bfloat16)
    shares = (
        lax.psum_scatter(query_mat_grad, ("dp", "fsdp"), scatter_dimension=0, tiled=True),
        lax.psum_scatter(query_vec_grad, ("dp", "fsdp"), scatter_dimension=0, tiled=True),
        lax.psum_scatter(key_mat_grad, ("dp", "fsdp"), scatter_dimension=0, tiled=True),
        lax.psum_scatter(value_mat_grad, ("dp", "fsdp"), scatter_dimension=0, tiled=True),
        lax.psum_scatter(value_vec_grad, ("dp", "fsdp"), scatter_dimension=0, tiled=True),
        lax.psum_scatter(output_mat_grad, ("dp", "fsdp"), scatter_dimension=0, tiled=True),
        lax.psum_scatter(output_vec_grad, ("dp", "fsdp"), scatter_dimension=0, tiled=True),
        lax.psum_scatter(first_gain_grad, ("dp", "fsdp"), scatter_dimension=0, tiled=True),
        lax.psum_scatter(first_shift_grad, ("dp", "fsdp"), scatter_dimension=0, tiled=True),
        lax.psum_scatter(inner_mat_grad, ("dp", "fsdp"), scatter_dimension=0, tiled=True),
        lax.psum_scatter(inner_vec_grad, ("dp", "fsdp"), scatter_dimension=0, tiled=True),
        lax.psum_scatter(outer_mat_grad, ("dp", "fsdp"), scatter_dimension=0, tiled=True),
        lax.psum_scatter(outer_vec_grad, ("dp", "fsdp"), scatter_dimension=0, tiled=True),
        lax.psum_scatter(second_gain_grad, ("dp", "fsdp"), scatter_dimension=0, tiled=True),
        lax.psum_scatter(second_shift_grad, ("dp", "fsdp"), scatter_dimension=0, tiled=True),
    )
    return (
        layer_out,
        frames_grad,
        shares[0],
        shares[1],
        shares[2],
        shares[3],
        shares[4],
        shares[5],
        shares[6],
        shares[7],
        shares[8],
        shares[9],
        shares[10],
        shares[11],
        shares[12],
        shares[13],
        shares[14],
    )


def solution(mesh):
    in_specs = (
        P(("dp", "fsdp"), None),
        P(("dp", "fsdp"), None),
        P(("dp", "fsdp"), None),
        P(("dp", "fsdp")),
        P(("dp", "fsdp"), None),
        P(("dp", "fsdp"), None),
        P(("dp", "fsdp")),
        P(("dp", "fsdp"), None),
        P(("dp", "fsdp")),
        P(("dp", "fsdp")),
        P(("dp", "fsdp")),
        P(("dp", "fsdp"), None),
        P(("dp", "fsdp")),
        P(("dp", "fsdp"), None),
        P(("dp", "fsdp")),
        P(("dp", "fsdp")),
        P(("dp", "fsdp")),
        P(("dp", "fsdp"), None),
    )
    out_specs = (
        P(("dp", "fsdp"), None),
        P(("dp", "fsdp"), None),
        P(("dp", "fsdp"), None),
        P(("dp", "fsdp")),
        P(("dp", "fsdp"), None),
        P(("dp", "fsdp"), None),
        P(("dp", "fsdp")),
        P(("dp", "fsdp"), None),
        P(("dp", "fsdp")),
        P(("dp", "fsdp")),
        P(("dp", "fsdp")),
        P(("dp", "fsdp"), None),
        P(("dp", "fsdp")),
        P(("dp", "fsdp"), None),
        P(("dp", "fsdp")),
        P(("dp", "fsdp")),
        P(("dp", "fsdp")),
    )
    return jax.shard_map(
        per_device, mesh=mesh, in_specs=in_specs, out_specs=out_specs, check_vma=False
    )
```

profile of v0, /device:TPU:0, one launch (start us, length us, event | category | flops | bytes accessed | tf_op | source)
XLA Modules:
  0.0 1126.1 jit_solution(13629870146439847360)
XLA Ops:
  11.2 0.8 dynamic-update-slice
  12.1 0.8 dynamic-update-slice.1
  12.9 0.8 dynamic-update-slice.2
  13.7 0.8 dynamic-update-slice.4
  14.6 0.8 dynamic-update-slice.3
  15.4 0.8 dynamic-update-slice.6
  16.2 0.8 dynamic-update-slice.8
  17.1 0.8 dynamic-update-slice.7
  17.9 0.8 dynamic-update-slice.5
  18.8 42.6 %all-reduce.19 = (bf16[768]{0:T(1024)(128)(2,1)S(1)}, bf16[768]{0:T(1024)(128)(2,1)S(1)}, bf16[768]{0:T(1024)(128)(2,1)S(1)}, bf16[768]{0:T(1024)(128)(2,1)S(1)}...) all-reduce(bf16[768]{0:T(1024)(128)(2,1)S(1)} %dynamic-update-slice, ...), channel_id=1, replica_groups=mesh['dp'=4,'fsdp'=8] {'dp','fsdp'}, use_global_device_ids=true, to_apply=%add | all-reduce | flops 9216 | bytes 36864
  61.4 1.3 fusion.35
  65.1 3.0 all-gather.7.cloned.1.call-done
  68.1 2.3 add_convert_fusion.3
  70.4 54.0 %all-gather.9.cloned.1.call-done = bf16[768,768]{1,0:T(8,128)(2,1)} async-done(((bf16[24,768]{1,0:T(8,128)(2,1)}), bf16[768,768]{1,0:T(8,128)(2,1)}) %all-gather.9.cloned.1.call-update) | async-done | bytes 1179664 | tf_op jit(solution)/shard_map/all_gather | solution.py:77
  124.4 2.9 add_convert_fusion.2
  127.6 1.7 copy.73
  129.3 51.2 %all-gather.11.cloned.1.call-done = bf16[768,768]{1,0:T(8,128)(2,1)} async-done(((bf16[24,768]{1,0:T(8,128)(2,1)}), bf16[768,768]{1,0:T(8,128)(2,1)}) %all-gather.11.cloned.1.call-update) | async-done | bytes 1179664 | tf_op jit(solution)/shard_map/all_gather | solution.py:79
  180.5 2.9 convolution_convert_fusion.1
  183.4 1.4 copy.74
  184.8 2.1 fusion.12
  186.9 2.6 fusion
  189.5 2.0 copy-done
  191.5 4.4 fusion.18
  195.8 40.6 %all-gather.13.cloned.1.call-done = bf16[768,768]{1,0:T(8,128)(2,1)} async-done(((bf16[24,768]{1,0:T(8,128)(2,1)}), bf16[768,768]{1,0:T(8,128)(2,1)}) %all-gather.13.cloned.1.call-update) | async-done | bytes 1179664 | tf_op jit(solution)/shard_map/all_gather | solution.py:82
  236.5 2.4 fusion.36
  238.9 1.1 copy-done.7
  240.4 61.6 %all-gather.15.cloned.1.call-done = bf16[768,3072]{1,0:T(8,128)(2,1)} async-done(((bf16[24,3072]{1,0:T(8,128)(2,1)}), bf16[768,3072]{1,0:T(8,128)(2,1)}) %all-gather.15.cloned.1.call-update) | async-done | bytes 4718608 | tf_op jit(solution)/shard_map/all_gather | solution.py:86
  301.9 21.0 %multiply_convert_fusion.1 = (bf16[512,3072]{1,0:T(8,128)(2,1)}, f32[512,3072]{1,0:T(8,128)}, f32[512,3072]{1,0:T(8,128)}) fusion(f32[3072]{0:T(1024)S(1)} %convert_element_type.159, bf16[768,3072]{1,0:T(8,128)(2,1)} %all-gather.15.cloned.1.call-done, f32[512,768]{1,0:T(8,128)} %copy-done.7, f32[768]{0:T(1024)S(1)} %convert_element_type.157, ...), kind=kOutput, calls=%fused_computation.14 | convolution fusion | flops 2521694208 | bytes 22042624 | tf_op jit(solution)/shard_map/dot_general | solution.py:20
  322.9 44.4 %all-gather.17.cloned.1.call-done = bf16[3072,768]{1,0:T(8,128)(2,1)} async-done(((bf16[96,768]{1,0:T(8,128)(2,1)}), bf16[3072,768]{1,0:T(8,128)(2,1)}) %all-gather.17.cloned.1.call-update) | async-done | bytes 4718608 | tf_op jit(solution)/shard_map/all_gather | solution.py:88
  367.3 6.1 fusion.37
  374.6 1.7 fusion.33
  377.2 8.5 convert_reduce_fusion
  385.7 3.1 multiply_reduce_fusion.2
  389.8 0.9 copy-done.14
  390.7 1.7 convolution_convert_fusion
  392.4 2.3 copy.76
  394.7 13.5 %multiply_reduce_fusion = (f32[12,512]{1,0:T(8,128)S(1)}, f32[12,512,512]{1,2,0:T(8,128)}) fusion(f32[12,512]{1,0:T(8,128)S(1)} %log_add_fusion, f32[12,512,512]{1,2,0:T(8,128)} %copy-done, pred[512,512]{0,1:T(8,128)(4,1)S(1)} %broadcast_compare_fusion, bf16[512,12,64]{0,2,1:T(8,128)(2,1)} %bitcast.82, bf16[512,12,64]{0,2,1:T(8,128)(2,1)} %bitcast.81), kind=kOutput, calls=%fused_computation.1 | convolution fusion | flops 418375680 | bytes 27049984 | tf_op jit(solution)/shard_map/qhd,khd->hqk/dot_general | solution.py:165
  408.3 7.0 multiply_convert_fusion
  415.3 1.2 convert_reduce_fusion.4
  416.5 1.4 copy-done.1
  417.9 0.9 copy-done.5
  418.8 2.2 convolution_bitcast_fusion.2
  421.0 3.1 copy.87
  424.4 4.8 multiply_convert_fusion.2
  429.2 0.9 copy-done.17
  430.1 2.2 convolution_bitcast_fusion.1
  432.3 3.2 copy.89
  435.6 6.6 convert_reduce_fusion.3
  442.2 0.9 copy-done.15
  443.1 2.2 convolution_bitcast_fusion
  445.3 3.2 copy.91
  448.6 3.7 fusion.40
  452.3 7.3 fusion.28
  459.7 1.1 copy-done.21
  460.7 8.2 fusion.41
  469.1 40.9 %all-reduce.18 = (f32[768]{0:T(1024)S(1)}, f32[768]{0:T(1024)S(1)}, f32[768]{0:T(1024)S(1)}, f32[768]{0:T(1024)S(1)}, f32[768]{0:T(1024)S(1)}, /*index=5*/f32[30...) all-reduce(f32[768]{0:T(1024)S(1)} %reduce_sum.228, ...), channel_id=3, replica_groups=mesh['dp'=4,'fsdp'=8] {'dp','fsdp'}, use_global_device_ids=true, to_apply=%region_14.15.clone | all-reduce | flops 9216 | bytes 73728
  515.3 2.2 fusion.39
  518.5 2.0 add_convert_fusion.1
  520.4 2.0 reduce-scatter.19.cloned.1.call-done
  522.4 104.8 %reduce-scatter.21.cloned.1.call-done = f32[24,768]{1,0:T(8,128)} async-done(((f32[768,768]{1,0:T(8,128)}), f32[24,768]{1,0:T(8,128)}) %reduce-scatter.21.cloned.1.call-update) | async-done | bytes 73744
  627.2 103.9 %reduce-scatter.23.cloned.1.call-done = f32[24,768]{1,0:T(8,128)} async-done(((f32[768,768]{1,0:T(8,128)}), f32[24,768]{1,0:T(8,128)}) %reduce-scatter.23.cloned.1.call-update) | async-done | bytes 73744
  731.2 104.6 %reduce-scatter.13.cloned.1.call-done = f32[24,768]{1,0:T(8,128)} async-done(((f32[768,768]{1,0:T(8,128)}), f32[24,768]{1,0:T(8,128)}) %reduce-scatter.13.cloned.1.call-update) | async-done | bytes 73744 | tf_op jit(solution)/shard_map/reduce_scatter | solution.py:204
  835.7 141.0 %reduce-scatter.15.cloned.1.call-done = f32[24,3072]{1,0:T(8,128)} async-done(((f32[768,3072]{1,0:T(8,128)}), f32[24,3072]{1,0:T(8,128)}) %reduce-scatter.15.cloned.1.call-update) | async-done | bytes 294928 | tf_op jit(solution)/shard_map/reduce_scatter | solution.py:208
  976.8 141.9 %reduce-scatter.17.cloned.1.call-done = f32[96,768]{1,0:T(8,128)} async-done(((f32[3072,768]{1,0:T(8,128)}), f32[96,768]{1,0:T(8,128)}) %reduce-scatter.17.cloned.1.call-update) | async-done | bytes 294928 | tf_op jit(solution)/shard_map/reduce_scatter | solution.py:210
  (130 shorter events, 15.3 us)
Async XLA Ops:
  7.2 117.2 %copy-start.2 = (bf16[512,768]{1,0:T(8,128)(2,1)S(1)}, bf16[512,768]{1,0:T(8,128)(2,1)}, u32[]{:S(2)}) copy-start(bf16[512,768]{1,0:T(8,128)(2,1)} %param.18) | copy-start | bytes 2359300
  7.2 60.9 %all-gather.7.cloned.1.call-start = ((), (), s32[]{:S(2)}) async-start(), calls=%async_computation.6 | async-start | bytes 1216512 | tf_op jit(solution)/shard_map/all_gather | solution.py:80
  7.9 116.4 %all-gather.9.cloned.1.call-start = ((), (), s32[]{:S(2)}) async-start(), calls=%async_computation.7 | async-start | bytes 1216512 | tf_op jit(solution)/shard_map/all_gather | solution.py:77
  8.7 171.8 %all-gather.11.cloned.1.call-start = ((), (), s32[]{:S(2)}) async-start(), calls=%async_computation.8 | async-start | bytes 1216512 | tf_op jit(solution)/shard_map/all_gather | solution.py:79
  9.4 227.0 %all-gather.13.cloned.1.call-start = ((), (), s32[]{:S(2)}) async-start(), calls=%async_computation.9 | async-start | bytes 1216512 | tf_op jit(solution)/shard_map/all_gather | solution.py:82
  10.0 292.0 %all-gather.15.cloned.1.call-start = ((), (), s32[]{:S(2)}) async-start(), calls=%async_computation.10 | async-start | bytes 4866048 | tf_op jit(solution)/shard_map/all_gather | solution.py:86
  10.6 356.7 %all-gather.17.cloned.1.call-start = ((), (), s32[]{:S(2)}) async-start(), calls=%async_computation.11 | async-start | bytes 4866048 | tf_op jit(solution)/shard_map/all_gather | solution.py:88
  11.2 511.3 %reduce-scatter.19.cloned.1.call-start = ((), (), s32[]{:S(2)}) async-start(), calls=%async_computation.15 | async-start | bytes 2433024
  127.6 61.9 %copy-start.11 = (bf16[512,768]{0,1:T(8,128)(2,1)}, bf16[512,768]{0,1:T(8,128)(2,1)S(1)}, u32[]{:S(2)}) copy-start(bf16[512,768]{0,1:T(8,128)(2,1)S(1)} %copy.72) | copy-start | bytes 2359300
  186.9 4.6 copy-start
  238.9 1.2 copy-start.7
  240.4 126.9 %copy-start.8 = (f32[512,768]{1,0:T(8,128)S(1)}, f32[512,768]{1,0:T(8,128)}, u32[]{:S(2)}) copy-start(f32[512,768]{1,0:T(8,128)} %copy-done.7) | copy-start | bytes 4718596
  367.3 6.4 copy-start.13
  374.6 2.6 copy-start.22
  376.3 9.4 slice-start.3
  376.5 9.2 copy-start.20
  377.2 8.5 slice-start.4
  385.7 3.2 copy-start.25
  385.7 3.2 copy-start.9
  388.9 1.8 copy-start.24
  389.8 0.9 copy-start.14
  394.7 13.5 %slice-start = ((s8[12582912]{0:T(1024)(128)(4,1)}), s8[4194304]{0:T(1024)(128)(4,1)S(1)}, s32[]{:S(2)}) async-start(s8[12582912]{0:T(1024)(128)(4,1)} %bitcast.72), calls=%async_computation.18 | async-start | bytes 8388608
  394.7 13.5 %slice-start.1 = ((s8[12582912]{0:T(1024)(128)(4,1)}), s8[4194304]{0:T(1024)(128)(4,1)S(1)}, s32[]{:S(2)}) async-start(s8[12582912]{0:T(1024)(128)(4,1)} %bitcast.72), calls=%async_computation.19 | async-start | bytes 8388608
  394.7 13.5 %slice-start.2 = ((s8[12582912]{0:T(1024)(128)(4,1)}), s8[4194304]{0:T(1024)(128)(4,1)S(1)}, s32[]{:S(2)}) async-start(s8[12582912]{0:T(1024)(128)(4,1)} %bitcast.72), calls=%async_computation.20 | async-start | bytes 8388608
  415.3 2.6 copy-start.1
  415.3 3.5 copy-start.3
  417.8 0.9 copy-start.5
  424.1 6.0 copy-start.4
  424.1 203.1 %reduce-scatter.21.cloned.1.call-start = ((), (), s32[]{:S(2)}) async-start(), calls=%async_computation.16 | async-start | bytes 2433024
  429.2 0.9 copy-start.17
  432.3 3.3 copy-start.12
  435.5 295.7 %reduce-scatter.23.cloned.1.call-start = ((), (), s32[]{:S(2)}) async-start(), calls=%async_computation.17 | async-start | bytes 2433024
  442.2 0.9 copy-start.15
  448.5 3.8 copy-start.10
  448.5 387.2 %reduce-scatter.13.cloned.1.call-start = ((), (), s32[]{:S(2)}) async-start(), calls=%async_computation.12 | async-start | bytes 2433024 | tf_op jit(solution)/shard_map/reduce_scatter | solution.py:204
  452.3 524.5 %reduce-scatter.15.cloned.1.call-start = ((), (), s32[]{:S(2)}) async-start(), calls=%async_computation.13 | async-start | bytes 9732096 | tf_op jit(solution)/shard_map/reduce_scatter | solution.py:208
  459.6 1.1 copy-start.21
  459.6 659.1 %reduce-scatter.17.cloned.1.call-start = ((), (), s32[]{:S(2)}) async-start(), calls=%async_computation.14 | async-start | bytes 9732096 | tf_op jit(solution)/shard_map/reduce_scatter | solution.py:210
  468.9 46.4 %copy-start.18 = (bf16[12,64,512]{2,1,0:T(8,128)(2,1)S(1)}, bf16[12,64,512]{2,1,0:T(8,128)(2,1)}, u32[]{:S(2)}) copy-start(bf16[12,64,512]{2,1,0:T(8,128)(2,1)} %copy-done.17) | copy-start | bytes 2359300
  469.0 48.6 %copy-start.6 = (bf16[12,64,512]{2,1,0:T(8,128)(2,1)S(1)}, bf16[12,64,512]{2,1,0:T(8,128)(2,1)}, u32[]{:S(2)}) copy-start(bf16[12,64,512]{2,1,0:T(8,128)(2,1)} %copy-done.5) | copy-start | bytes 2359300
  510.1 7.5 copy-start.23
  515.3 3.1 copy-start.16
  515.3 3.1 copy-start.19
Sparse Core Ops, SparseCore 0:
  11.0 57.0 all-gather.6
  71.1 53.2 all-gather.8
  127.4 53.0 all-gather.10
  183.3 53.0 all-gather.12
  239.3 62.6 all-gather.14
  304.8 62.4 all-gather.16
  424.2 98.1 reduce-scatter.18
  529.1 98.0 reduce-scatter.20
  633.1 98.0 reduce-scatter.22
  737.7 97.9 reduce-scatter.12
  842.2 134.5 reduce-scatter.14
  984.1 134.5 reduce-scatter.16
where the time goes:
time: 1140 us; the launch traced here: 1130 us
  waiting for transfers between devices  857 us (75%)
  matrix products  114 us (10%)
  blocking collectives  83.5 us (7%)
  local copies, waits for them, and re-layouts  39.3 us (3%)
  between operations  16.5 us (1%)
  other arithmetic  14.8 us (1%)
    unnamed x15, waiting for transfers between devices  214 us
    reduce_scatter x1, waiting for transfers between devices, per_device(): lax.psum_scatter(outer_mat_grad, ('dp', 'fsdp'), scatter_dimension=0, til...  142 us
    reduce_scatter x1, waiting for transfers between devices, per_device(): lax.psum_scatter(inner_mat_grad, ('dp', 'fsdp'), scatter_dimension=0, til...  141 us
    reduce_scatter x1, waiting for transfers between devices, per_device(): lax.psum_scatter(output_mat_grad, ('dp', 'fsdp'), scatter_dimension=0, ti...  105 us
    unnamed x2, blocking collectives  83.5 us
    all_gather x1, waiting for transfers between devices, per_device(): lax.all_gather(inner_weight, ('dp', 'fsdp'), axis=0, tiled=True)  61.6 us
    all_gather x1, waiting for transfers between devices, per_device(): lax.all_gather(query_weight, ('dp', 'fsdp'), axis=0, tiled=True)  54 us
    all_gather x1, waiting for transfers between devices, per_device(): lax.all_gather(key_weight, ('dp', 'fsdp'), axis=0, tiled=True)  51.2 us
  transfers between devices with their start and end apart: 12, of which 12 were waited for; matrix products, arithmetic and copies ran while one was open for 9% of the time, Pallas kernels for 0%

commit v1 on v0

--- a/solution.py
+++ b/solution.py
@@ -4,6 +4,27 @@
 from jax.sharding import PartitionSpec as P
 
 HEADS = 12
+
+
+def boxes_cut(u_in, at_axis):
+    placed = list(u_in.shape[1:])
+    placed[at_axis] *= u_in.shape[0]
+    vec_out = jnp.moveaxis(u_in, 0, at_axis).reshape(placed)
+    return vec_out
+
+
+def mark_numbers(arr, along_axis):
+    n_parts = lax.axis_size(along_axis)
+    piece_out = arr[None]
+    for hop_no in range(n_parts.bit_length() - 1):
+        step_out = 1 << hop_no
+        opened = lax.ppermute(
+            piece_out, along_axis, list(map(lambda it: (it, it ^ step_out), range(n_parts)))
+        )
+        seen_now = jnp.stack([piece_out, opened], axis=0)
+        far_arr = lax.axis_index(along_axis) >> hop_no & 1
+        piece_out = jnp.where(far_arr == 0, seen_now, seen_now[::-1]).reshape(-1, *arr.shape)
+    return piece_out
 
 
 def layer_norm(values, gain_vec, shift_vec):
@@ -73,13 +94,18 @@
     bounds = jnp.stack([lengths[0, 0], lengths[0, 0] + lengths[0, 1]])
     groups = jnp.sum((places[:, None] >= bounds[None, :]).astype(jnp.int32), axis=1)
     live_mask = (places < bounds[-1]).astype(jnp.float32)
+
+    def trace_the_scales(base_x, work_x, along_dim):
+        front = boxes_cut(mark_numbers(base_x, work_x), along_dim)
+        return front
+
     gathered = (
         lax.all_gather(query_weight, ("dp", "fsdp"), axis=0, tiled=True),
         lax.all_gather(query_bias, ("dp", "fsdp"), axis=0, tiled=True),
         lax.all_gather(key_weight, ("dp", "fsdp"), axis=0, tiled=True),
         lax.all_gather(value_weight, ("dp", "fsdp"), axis=0, tiled=True),
         lax.all_gather(value_bias, ("dp", "fsdp"), axis=0, tiled=True),
-        lax.all_gather(output_weight, ("dp", "fsdp"), axis=0, tiled=True),
+        trace_the_scales(output_weight, ("dp", "fsdp"), 0),
         lax.all_gather(output_bias, ("dp", "fsdp"), axis=0, tiled=True),
         lax.all_gather(first_gain, ("dp", "fsdp"), axis=0, tiled=True),
         lax.all_gather(first_shift, ("dp", "fsdp"), axis=0, tiled=True),

time: 1140 us -> 1080 us (0.947)
  waiting for transfers between devices: 857 us -> 795 us
    all_gather x1 -> x0, waiting for transfers between devices: 40.6 us -> none  [per_device(): lax.all_gather(output_weight, ('dp', 'fsdp'), axis=0, tiled=True)]
    all_gather x1, waiting for transfers between devices: 54 us -> 38.2 us  [per_device(): lax.all_gather(query_weight, ('dp', 'fsdp'), axis=0, tiled=True)]
    all_gather x1, waiting for transfers between devices: 61.6 us -> 48.5 us  [per_device(): lax.all_gather(inner_weight, ('dp', 'fsdp'), axis=0, tiled=True)]
    unnamed x92 -> x116, local copies, waits for them, and re-layouts: 32.1 us -> 26.6 us
    unnamed x15 -> x14, waiting for transfers between devices: 214 us -> 214 us
  transfers between devices with their start and end apart: 12 -> 16, of which waited for: 12 -> 14; matrix products, arithmetic and copies ran while one was open for 9% -> 9% of each run, Pallas kernels for 0% -> 0%
where the time goes in v1:
time: 1080 us; the launch traced here: 1070 us
  waiting for transfers between devices  795 us (74%)
  matrix products  112 us (10%)
  blocking collectives  87.2 us (8%)
  local copies, waits for them, and re-layouts  33.1 us (3%)
  other arithmetic  17.3 us (2%)
  between operations  16.1 us (1%)
  starting transfers between devices  10.9 us (1%)
    unnamed x14, waiting for transfers between devices  214 us
    reduce_scatter x1, waiting for transfers between devices, per_device(): lax.psum_scatter(outer_mat_grad, ('dp', 'fsdp'), scatter_dimension=0, til...  142 us
    reduce_scatter x1, waiting for transfers between devices, per_device(): lax.psum_scatter(inner_mat_grad, ('dp', 'fsdp'), scatter_dimension=0, til...  141 us
    reduce_scatter x1, waiting for transfers between devices, per_device(): lax.psum_scatter(output_mat_grad, ('dp', 'fsdp'), scatter_dimension=0, ti...  105 us
    unnamed x2, blocking collectives  87.2 us
    all_gather x1, waiting for transfers between devices, per_device(): lax.all_gather(key_weight, ('dp', 'fsdp'), axis=0, tiled=True)  51.2 us
    all_gather x1, waiting for transfers between devices, per_device(): lax.all_gather(inner_weight, ('dp', 'fsdp'), axis=0, tiled=True)  48.5 us
    all_gather x1, waiting for transfers between devices, per_device(): lax.all_gather(outer_weight, ('dp', 'fsdp'), axis=0, tiled=True)  44.3 us
  transfers between devices with their start and end apart: 16, of which 14 were waited for; matrix products, arithmetic and copies ran while one was open for 9% of the time, Pallas kernels for 0%

profile of v1, /device:TPU:0, one launch (start us, length us, event | category | flops | bytes accessed | tf_op | source)
XLA Modules:
  0.0 1071.4 jit_solution(13943416034005737071)
XLA Ops:
  10.1 3.0 collective-permute-start
  13.1 2.1 collective-permute-done
  15.3 0.8 pad_maximum_fusion.4
  16.1 2.2 collective-permute-start.1
  18.3 2.3 collective-permute-done.1
  20.6 3.1 collective-permute-start.2
  23.7 5.0 collective-permute-done.2
  29.0 1.5 collective-permute-done.3
  30.6 1.9 collective-permute-start.4
  35.3 46.4 %all-reduce.19 = (bf16[768]{0:T(1024)(128)(2,1)S(1)}, bf16[768]{0:T(1024)(128)(2,1)S(1)}, bf16[768]{0:T(1024)(128)(2,1)S(1)}, bf16[768]{0:T(1024)(128)(2,1)S(1)}...) all-reduce(bf16[768]{0:T(1024)(128)(2,1)S(1)} %dynamic-update-slice, ...), channel_id=1, replica_groups=mesh['dp'=4,'fsdp'=8] {'dp','fsdp'}, use_global_device_ids=true, to_apply=%add | all-reduce | flops 9216 | bytes 36864
  84.2 1.3 reverse_select_fusion
  85.5 2.1 add_convert_fusion.3
  87.6 38.2 %all-gather.8.cloned.1.call-done = bf16[768,768]{1,0:T(8,128)(2,1)} async-done(((bf16[24,768]{1,0:T(8,128)(2,1)}), bf16[768,768]{1,0:T(8,128)(2,1)}) %all-gather.8.cloned.1.call-update) | async-done | bytes 1179664 | tf_op jit(solution)/shard_map/all_gather | solution.py:103
  125.8 2.9 add_convert_fusion.2
  129.0 1.7 copy.73
  130.7 51.2 %all-gather.10.cloned.1.call-done = bf16[768,768]{1,0:T(8,128)(2,1)} async-done(((bf16[24,768]{1,0:T(8,128)(2,1)}), bf16[768,768]{1,0:T(8,128)(2,1)}) %all-gather.10.cloned.1.call-update) | async-done | bytes 1179664 | tf_op jit(solution)/shard_map/all_gather | solution.py:105
  181.9 2.9 convolution_convert_fusion.1
  184.8 1.4 copy.74
  186.2 2.1 fusion.12
  188.3 2.6 fusion
  190.9 1.9 copy-done
  192.8 3.6 fusion.18
  196.4 0.9 fusion.38
  197.4 1.1 copy-done.7
  198.8 48.5 %all-gather.12.cloned.1.call-done = bf16[768,3072]{1,0:T(8,128)(2,1)} async-done(((bf16[24,3072]{1,0:T(8,128)(2,1)}), bf16[768,3072]{1,0:T(8,128)(2,1)}) %all-gather.12.cloned.1.call-update) | async-done | bytes 4718608 | tf_op jit(solution)/shard_map/all_gather | solution.py:112
  247.4 21.0 %multiply_convert_fusion.1 = (bf16[512,3072]{1,0:T(8,128)(2,1)}, f32[512,3072]{1,0:T(8,128)}, f32[512,3072]{1,0:T(8,128)}) fusion(f32[3072]{0:T(1024)S(1)} %convert_element_type.161, bf16[768,3072]{1,0:T(8,128)(2,1)} %all-gather.12.cloned.1.call-done, f32[512,768]{1,0:T(8,128)} %copy-done.7, f32[768]{0:T(1024)S(1)} %convert_element_type.159, ...), kind=kOutput, calls=%fused_computation.14 | convolution fusion | flops 2521694208 | bytes 22042624 | tf_op jit(solution)/shard_map/dot_general | solution.py:41
  268.4 44.3 %all-gather.14.cloned.1.call-done = bf16[3072,768]{1,0:T(8,128)(2,1)} async-done(((bf16[96,768]{1,0:T(8,128)(2,1)}), bf16[3072,768]{1,0:T(8,128)(2,1)}) %all-gather.14.cloned.1.call-update) | async-done | bytes 4718608 | tf_op jit(solution)/shard_map/all_gather | solution.py:114
  312.7 6.1 fusion.39
  319.2 0.8 multiply_reduce_fusion.1
  320.0 1.7 fusion.35
  322.6 8.7 convert_reduce_fusion
  331.3 3.2 multiply_reduce_fusion.2
  335.4 0.9 copy-done.14
  336.3 1.7 convolution_convert_fusion
  338.0 2.3 copy.76
  340.3 13.5 %multiply_reduce_fusion = (f32[12,512]{1,0:T(8,128)S(1)}, f32[12,512,512]{1,2,0:T(8,128)}) fusion(f32[12,512]{1,0:T(8,128)S(1)} %log_add_fusion, f32[12,512,512]{1,2,0:T(8,128)} %copy-done, pred[512,512]{0,1:T(8,128)(4,1)S(1)} %broadcast_compare_fusion, bf16[512,12,64]{0,2,1:T(8,128)(2,1)} %bitcast.100, bf16[512,12,64]{0,2,1:T(8,128)(2,1)} %bitcast.99), kind=kOutput, calls=%fused_computation.1 | convolution fusion | flops 418375680 | bytes 27049984 | tf_op jit(solution)/shard_map/qhd,khd->hqk/dot_general | solution.py:191
  353.9 7.0 multiply_convert_fusion
  360.9 1.2 convert_reduce_fusion.4
  362.1 1.4 copy-done.1
  363.5 0.9 copy-done.5
  364.4 2.2 convolution_bitcast_fusion.2
  366.6 3.0 copy.87
  369.9 4.8 multiply_convert_fusion.2
  374.8 0.9 copy-done.17
  375.6 2.2 convolution_bitcast_fusion.1
  377.8 3.2 copy.89
  381.0 6.6 convert_reduce_fusion.3
  387.7 0.9 copy-done.15
  388.6 2.2 convolution_bitcast_fusion
  390.8 3.1 copy.91
  394.0 3.7 fusion.42
  397.8 7.3 fusion.30
  405.1 1.1 copy-done.23
  406.2 8.2 fusion.43
  414.6 40.8 %all-reduce.18 = (f32[768]{0:T(1024)S(1)}, f32[768]{0:T(1024)S(1)}, f32[768]{0:T(1024)S(1)}, f32[768]{0:T(1024)S(1)}, f32[768]{0:T(1024)S(1)}, /*index=5*/f32[30...) all-reduce(f32[768]{0:T(1024)S(1)} %reduce_sum.228, ...), channel_id=3, replica_groups=mesh['dp'=4,'fsdp'=8] {'dp','fsdp'}, use_global_device_ids=true, to_apply=%region_14.15.clone | all-reduce | flops 9216 | bytes 73728
  460.6 2.2 fusion.41
  462.9 0.8 fusion.40
  463.8 2.0 add_convert_fusion.1
  465.7 2.4 reduce-scatter.19.cloned.1.call-done
  468.1 104.8 %reduce-scatter.21.cloned.1.call-done = f32[24,768]{1,0:T(8,128)} async-done(((f32[768,768]{1,0:T(8,128)}), f32[24,768]{1,0:T(8,128)}) %reduce-scatter.21.cloned.1.call-update) | async-done | bytes 73744
  572.9 103.9 %reduce-scatter.23.cloned.1.call-done = f32[24,768]{1,0:T(8,128)} async-done(((f32[768,768]{1,0:T(8,128)}), f32[24,768]{1,0:T(8,128)}) %reduce-scatter.23.cloned.1.call-update) | async-done | bytes 73744
  676.8 104.8 %reduce-scatter.13.cloned.1.call-done = f32[24,768]{1,0:T(8,128)} async-done(((f32[768,768]{1,0:T(8,128)}), f32[24,768]{1,0:T(8,128)}) %reduce-scatter.13.cloned.1.call-update) | async-done | bytes 73744 | tf_op jit(solution)/shard_map/reduce_scatter | solution.py:230
  781.6 140.8 %reduce-scatter.15.cloned.1.call-done = f32[24,3072]{1,0:T(8,128)} async-done(((f32[768,3072]{1,0:T(8,128)}), f32[24,3072]{1,0:T(8,128)}) %reduce-scatter.15.cloned.1.call-update) | async-done | bytes 294928 | tf_op jit(solution)/shard_map/reduce_scatter | solution.py:234
  922.5 142.2 %reduce-scatter.17.cloned.1.call-done = f32[96,768]{1,0:T(8,128)} async-done(((f32[3072,768]{1,0:T(8,128)}), f32[96,768]{1,0:T(8,128)}) %reduce-scatter.17.cloned.1.call-update) | async-done | bytes 294928 | tf_op jit(solution)/shard_map/reduce_scatter | solution.py:236
  (171 shorter events, 15.7 us)
Async XLA Ops:
  7.2 25.4 %copy-start.25 = (s32[1,2]{1,0:T(1,128)S(1)}, s32[1,2]{1,0:T(1,128)}, u32[]{:S(2)}) copy-start(s32[1,2]{1,0:T(1,128)} %param.19) | copy-start | bytes 28
  7.2 26.0 %copy-start.28 = (bf16[24]{0:T(256)(128)(2,1)S(1)}, bf16[24]{0:T(256)(128)(2,1)}, u32[]{:S(2)}) copy-start(bf16[24]{0:T(256)(128)(2,1)} %param.24) | copy-start | bytes 148
  7.2 26.2 %copy-start.29 = (bf16[24]{0:T(256)(128)(2,1)S(1)}, bf16[24]{0:T(256)(128)(2,1)}, u32[]{:S(2)}) copy-start(bf16[24]{0:T(256)(128)(2,1)} %param.21) | copy-start | bytes 148
  7.2 26.4 %copy-start.30 = (bf16[24]{0:T(256)(128)(2,1)S(1)}, bf16[24]{0:T(256)(128)(2,1)}, u32[]{:S(2)}) copy-start(bf16[24]{0:T(256)(128)(2,1)} %param.26) | copy-start | bytes 148
  7.2 26.6 %copy-start.31 = (bf16[24]{0:T(256)(128)(2,1)S(1)}, bf16[24]{0:T(256)(128)(2,1)}, u32[]{:S(2)}) copy-start(bf16[24]{0:T(256)(128)(2,1)} %param.28) | copy-start | bytes 148
  7.2 26.9 %copy-start.32 = (bf16[24]{0:T(256)(128)(2,1)S(1)}, bf16[24]{0:T(256)(128)(2,1)}, u32[]{:S(2)}) copy-start(bf16[24]{0:T(256)(128)(2,1)} %param.27) | copy-start | bytes 148
  7.2 27.1 %copy-start.33 = (bf16[24]{0:T(256)(128)(2,1)S(1)}, bf16[24]{0:T(256)(128)(2,1)}, u32[]{:S(2)}) copy-start(bf16[24]{0:T(256)(128)(2,1)} %param.32) | copy-start | bytes 148
  7.3 27.3 %copy-start.34 = (bf16[24]{0:T(256)(128)(2,1)S(1)}, bf16[24]{0:T(256)(128)(2,1)}, u32[]{:S(2)}) copy-start(bf16[24]{0:T(256)(128)(2,1)} %param.34) | copy-start | bytes 148
  7.3 27.5 %copy-start.35 = (bf16[24]{0:T(256)(128)(2,1)S(1)}, bf16[24]{0:T(256)(128)(2,1)}, u32[]{:S(2)}) copy-start(bf16[24]{0:T(256)(128)(2,1)} %param.33) | copy-start | bytes 148
  7.3 27.8 %copy-start.36 = (bf16[96]{0:T(256)(128)(2,1)S(1)}, bf16[96]{0:T(256)(128)(2,1)}, u32[]{:S(2)}) copy-start(bf16[96]{0:T(256)(128)(2,1)} %param.30) | copy-start | bytes 580
  7.3 78.2 %all-gather.6.cloned.1.call-start = ((), (), s32[]{:S(2)}) async-start(), calls=%async_computation.6 | async-start | bytes 1216512 | tf_op jit(solution)/shard_map/all_gather | solution.py:106
  8.0 117.7 %all-gather.8.cloned.1.call-start = ((), (), s32[]{:S(2)}) async-start(), calls=%async_computation.7 | async-start | bytes 1216512 | tf_op jit(solution)/shard_map/all_gather | solution.py:103
  8.8 173.1 %all-gather.10.cloned.1.call-start = ((), (), s32[]{:S(2)}) async-start(), calls=%async_computation.8 | async-start | bytes 1216512 | tf_op jit(solution)/shard_map/all_gather | solution.py:105
  9.5 237.9 %all-gather.12.cloned.1.call-start = ((), (), s32[]{:S(2)}) async-start(), calls=%async_computation.9 | async-start | bytes 4866048 | tf_op jit(solution)/shard_map/all_gather | solution.py:112
  10.1 302.6 %all-gather.14.cloned.1.call-start = ((), (), s32[]{:S(2)}) async-start(), calls=%async_computation.10 | async-start | bytes 4866048 | tf_op jit(solution)/shard_map/all_gather | solution.py:114
  10.1 5.2 collective-permute-start
  16.1 4.5 collective-permute-start.1
  20.6 8.1 collective-permute-start.2
  28.8 1.6 collective-permute-start.3
  28.9 439.2 %reduce-scatter.19.cloned.1.call-start = ((), (), s32[]{:S(2)}) async-start(), calls=%async_computation.14 | async-start | bytes 2433024
  30.5 55.0 %copy-start.2 = (bf16[512,768]{1,0:T(8,128)(2,1)S(1)}, bf16[512,768]{1,0:T(8,128)(2,1)}, u32[]{:S(2)}) copy-start(bf16[512,768]{1,0:T(8,128)(2,1)} %param.18) | copy-start | bytes 2359300
  30.6 53.5 %collective-permute-start.4 = (bf16[16,24,768]{2,1,0:T(8,128)(2,1)S(1)}, bf16[16,24,768]{2,1,0:T(8,128)(2,1)S(1)}, u32[]{:S(2)}, u32[]{:S(2)}) collective-permute-start(bf16[16,24,768]{2,1,0:T(8,128)(2,1)S(1)} %bitcast.106), channel_id=1, source_target_pairs={{0,16},{1,17},{2,18},{3,19},{4,20},{5,21},{6,22},{7,23},{8,24},{9,... | collective-permute-start | bytes 1769480 | tf_op jit(solution)/shard_map/ppermute | solution.py:21
  129.0 61.9 %copy-start.11 = (bf16[512,768]{0,1:T(8,128)(2,1)}, bf16[512,768]{0,1:T(8,128)(2,1)S(1)}, u32[]{:S(2)}) copy-start(bf16[512,768]{0,1:T(8,128)(2,1)S(1)} %copy.72) | copy-start | bytes 2359300
  188.3 4.5 copy-start
  192.8 3.6 copy-start.19
  196.4 2.4 copy-start.24
  197.4 1.1 copy-start.7
  198.8 113.9 %copy-start.8 = (f32[512,768]{1,0:T(8,128)S(1)}, f32[512,768]{1,0:T(8,128)}, u32[]{:S(2)}) copy-start(f32[512,768]{1,0:T(8,128)} %copy-done.7) | copy-start | bytes 4718596
  312.7 6.4 copy-start.13
  320.0 2.6 copy-start.26
  321.7 9.6 slice-start.3
  321.9 9.4 copy-start.22
  322.6 8.7 slice-start.4
  331.3 3.2 copy-start.37
  331.3 3.2 copy-start.9
  334.5 1.8 copy-start.20
  335.4 0.9 copy-start.14
  340.3 13.5 %slice-start = ((s8[12582912]{0:T(1024)(128)(4,1)}), s8[4194304]{0:T(1024)(128)(4,1)S(1)}, s32[]{:S(2)}) async-start(s8[12582912]{0:T(1024)(128)(4,1)} %bitcast.90), calls=%async_computation.17 | async-start | bytes 8388608
  340.3 13.5 %slice-start.1 = ((s8[12582912]{0:T(1024)(128)(4,1)}), s8[4194304]{0:T(1024)(128)(4,1)S(1)}, s32[]{:S(2)}) async-start(s8[12582912]{0:T(1024)(128)(4,1)} %bitcast.90), calls=%async_computation.18 | async-start | bytes 8388608
  340.3 13.5 %slice-start.2 = ((s8[12582912]{0:T(1024)(128)(4,1)}), s8[4194304]{0:T(1024)(128)(4,1)S(1)}, s32[]{:S(2)}) async-start(s8[12582912]{0:T(1024)(128)(4,1)} %bitcast.90), calls=%async_computation.19 | async-start | bytes 8388608
  360.9 2.6 copy-start.1
  360.9 3.5 copy-start.3
  363.5 0.9 copy-start.5
  369.7 5.9 copy-start.4
  369.7 203.2 %reduce-scatter.21.cloned.1.call-start = ((), (), s32[]{:S(2)}) async-start(), calls=%async_computation.15 | async-start | bytes 2433024
  374.7 0.9 copy-start.17
  377.8 3.2 copy-start.12
  381.0 295.8 %reduce-scatter.23.cloned.1.call-start = ((), (), s32[]{:S(2)}) async-start(), calls=%async_computation.16 | async-start | bytes 2433024
  387.7 0.9 copy-start.15
  394.0 3.8 copy-start.10
  394.0 387.6 %reduce-scatter.13.cloned.1.call-start = ((), (), s32[]{:S(2)}) async-start(), calls=%async_computation.11 | async-start | bytes 2433024 | tf_op jit(solution)/shard_map/reduce_scatter | solution.py:230
  397.7 524.7 %reduce-scatter.15.cloned.1.call-start = ((), (), s32[]{:S(2)}) async-start(), calls=%async_computation.12 | async-start | bytes 9732096 | tf_op jit(solution)/shard_map/reduce_scatter | solution.py:234
  405.0 1.1 copy-start.23
  405.1 659.6 %reduce-scatter.17.cloned.1.call-start = ((), (), s32[]{:S(2)}) async-start(), calls=%async_computation.13 | async-start | bytes 9732096 | tf_op jit(solution)/shard_map/reduce_scatter | solution.py:236
  414.4 46.2 %copy-start.18 = (bf16[12,64,512]{2,1,0:T(8,128)(2,1)S(1)}, bf16[12,64,512]{2,1,0:T(8,128)(2,1)}, u32[]{:S(2)}) copy-start(bf16[12,64,512]{2,1,0:T(8,128)(2,1)} %copy-done.17) | copy-start | bytes 2359300
  414.4 48.5 %copy-start.6 = (bf16[12,64,512]{2,1,0:T(8,128)(2,1)S(1)}, bf16[12,64,512]{2,1,0:T(8,128)(2,1)}, u32[]{:S(2)}) copy-start(bf16[12,64,512]{2,1,0:T(8,128)(2,1)} %copy-done.5) | copy-start | bytes 2359300
  455.4 7.5 copy-start.27
  460.6 3.1 copy-start.16
  460.6 3.1 copy-start.21
Sparse Core Ops, SparseCore 0:
  11.1 58.5 all-gather.5
  72.6 53.0 all-gather.7
  128.8 53.0 all-gather.9
  184.7 62.6 all-gather.11
  250.2 62.4 all-gather.13
  369.8 98.2 reduce-scatter.18
  474.8 98.0 reduce-scatter.20
  578.8 97.9 reduce-scatter.22
  683.5 98.0 reduce-scatter.12
  787.9 134.4 reduce-scatter.14
  929.9 134.6 reduce-scatter.16
